TPU v7x, 32 devices: a whole 2x2x4 slice. The times are simulated.
32 devices in a mesh: case: 2 (over y), blk: 4 (over z), split: 2 (over x), sub: 2 (over core).
Axes of the slice: x: 2, y: 2, z: 4, core: 2. Of those that a mesh axis runs over, the one named last changes fastest.
Arguments:
- cell_series: bfloat16 [32768, 4, 512], P(('case', 'blk', 'split', 'sub')), parts along dimension 0, may hold values from -6 to 6
- cell_count: int32 [32], P(('case', 'blk', 'split', 'sub')), parts along dimension 0, may hold values from 768 to 1024, as said below
- cell_target: int32 [32768], P(('case', 'blk', 'split', 'sub')), parts along dimension 0, may hold values from 0 to 2047, as said below
- surface: float32 [4, 8192], P(None, ('case', 'blk', 'split', 'sub')), parts along dimension 1, may hold values from -8.5 to 16.5, as said below
- observers: float32 [3, 1024], P(None, 'case'), parts along dimension 1, may hold values from -45 to 53, as said below
Outputs:
- pressure: float32 [1024, 2, 8], P(('case', 'blk')), parts along dimension 0
There are 2 independent parts, one for each index of `case`. A program takes and returns all parts, laid end to end along the dimension named above; each array names one. Nothing has to cross between parts.
Inputs may be any that keep to these rules, and one draw needn't show every extreme that they name: Cells i of a device with i < cell_count are live. `cell_target`: an entry t names local surface point t mod 256 of the device whose index along blk+split is t // 256 and whose sub index is the cell's. Among the rows of one device no such owner is named more than 192 times; in every device one owner is named by exactly 192 live rows, the same owner for all devices of one sub index. Every surface point lies within 8.5 of the point (8, 0, 0); panel areas are positive. `observers`: every observer lies 18 or more from the point (8, 0, 0).
All inputs are finite; a program needn't handle non-finite values.
Results may differ from a plain program's by a relative error of at most 0.0027.
Values may be sent and summed in bfloat16 or wider, within the bound.
A program may use at most 64 MiB of HBM per device.

v0:
```python
import math
import jax
import jax.numpy as jnp
from jax import lax
from jax.sharding import PartitionSpec as P

NF = 8


def spectral_lookup_matrix(signal_readings):
    clock_moments = jnp.arange(signal_readings, dtype=jnp.int32)
    spectral_slot_number = jnp.arange(NF, dtype=jnp.int32) + signal_readings // 16
    modulo_angle_value = spectral_slot_number[:, None] * clock_moments[None, :] % signal_readings
    phases = 2.0 * math.pi / signal_readings * modulo_angle_value.astype(jnp.float32)
    hann_attenuation_curve = 0.5 - 0.5 * jnp.cos(
        2.0 * math.pi / signal_readings * clock_moments.astype(jnp.float32)
    )
    scaled = 2.0 / signal_readings * hann_attenuation_curve[None, :]
    return jnp.concatenate([scaled * jnp.cos(phases), -scaled * jnp.sin(phases)], axis=0).astype(
        jnp.bfloat16
    )


def radiate(spectra, surface, listeners, amplitude):
    delta_x = listeners[0][:, None] - surface[0][None, :]
    delta_y = listeners[1][:, None] - surface[1][None, :]
    delta_z = listeners[2][:, None] - surface[2][None, :]
    radius = jnp.sqrt(delta_x * delta_x + delta_y * delta_y + delta_z * delta_z)
    inverse = 1.0 / radius
    normal_x = delta_x * inverse
    normal_y = delta_y * inverse
    normal_z = delta_z * inverse
    quadrature_factor = surface[3][None, :] * inverse * (amplitude / (4.0 * math.pi))
    blocks = spectra.reshape(2, NF, 4, spectra.shape[1])
    real_list = []
    imag_list = []
    for harmonic in range(NF):
        wavenumber = 0.5 + 0.25 * harmonic
        real_part = blocks[0, harmonic]
        imag_part = blocks[1, harmonic]
        load_real = (
            real_part[1][None, :] * normal_x
            + real_part[2][None, :] * normal_y
            + real_part[3][None, :] * normal_z
        )
        load_imag = (
            imag_part[1][None, :] * normal_x
            + imag_part[2][None, :] * normal_y
            + imag_part[3][None, :] * normal_z
        )
        source_real = (
            -wavenumber * imag_part[0][None, :] + load_real * inverse - wavenumber * load_imag
        )
        source_imag = (
            wavenumber * real_part[0][None, :] + wavenumber * load_real + load_imag * inverse
        )
        cosine = jnp.cos(wavenumber * radius)
        sinusoid = jnp.sin(wavenumber * radius)
        real_list.append(
            jnp.sum(quadrature_factor * (source_real * cosine + source_imag * sinusoid), axis=1)
        )
        imag_list.append(
            jnp.sum(quadrature_factor * (source_imag * cosine - source_real * sinusoid), axis=1)
        )
    real_out = jnp.stack(real_list, axis=1)
    imag_out = jnp.stack(imag_list, axis=1)
    return jnp.stack([real_out, imag_out], axis=1)


def local(cell_series, cell_count, cell_target, surface, observers):
    rows_dev = cell_series.shape[0]
    signal_readings = cell_series.shape[2]
    points_dev = surface.shape[1]
    source_groups = lax.axis_size("blk") * lax.axis_size("split")
    devices = source_groups * lax.axis_size("sub")
    capacity = (3 * rows_dev + 2 * source_groups - 1) // (2 * source_groups)
    slot_total = source_groups * capacity
    amplitude = 150.0 * math.sqrt(
        signal_readings * points_dev / (rows_dev * (points_dev * devices))
    )
    twiddle = spectral_lookup_matrix(signal_readings)
    row_index = jnp.arange(rows_dev, dtype=jnp.int32)
    active = row_index < cell_count[0]
    owner_index = cell_target // points_dev
    point_index = cell_target % points_dev
    matches = (
        (owner_index[:, None] == jnp.arange(source_groups, dtype=jnp.int32)[None, :])
        & active[:, None]
    ).astype(jnp.int32)
    sorted_ranking = jnp.sum(jnp.cumsum(matches, axis=0) * matches, axis=1) - 1
    destination = jnp.where(active, owner_index * capacity + sorted_ranking, slot_total)
    slot_source = (
        jnp.full((slot_total + 1,), rows_dev, jnp.int32).at[destination].set(row_index)[:slot_total]
    )
    slot_point = jnp.take(point_index, slot_source, mode="fill", fill_value=-1)
    flattened = cell_series.reshape(rows_dev * 4, signal_readings)
    per_cell = jnp.einsum("jt,rt->jr", twiddle, flattened, preferred_element_type=jnp.float32)
    per_cell = per_cell.reshape(2 * NF, rows_dev, 4).transpose(1, 0, 2).reshape(rows_dev, 8 * NF)
    outgoing = jnp.take(per_cell, slot_source, axis=0, mode="fill", fill_value=0.0)
    arrived_points, arrived = (
        lax.all_to_all(
            slot_point.reshape(source_groups, capacity),
            ("blk", "split"),
            split_axis=0,
            concat_axis=0,
            tiled=True,
        ),
        lax.all_to_all(
            outgoing.reshape(source_groups, capacity, 8 * NF),
            ("blk", "split"),
            split_axis=0,
            concat_axis=0,
            tiled=True,
        ),
    )
    arrived_points = arrived_points.reshape(slot_total)
    placing = (arrived_points[:, None] == jnp.arange(points_dev, dtype=jnp.int32)[None, :]).astype(
        jnp.float32
    )
    spectra = jnp.dot(
        arrived.reshape(slot_total, 8 * NF).T,
        placing,
        precision=lax.Precision.HIGHEST,
        preferred_element_type=jnp.float32,
    )
    summed = lax.psum_scatter(
        radiate(spectra, surface, observers, amplitude), "blk", scatter_dimension=0, tiled=True
    )
    return lax.psum(summed, ("split", "sub"))


def solution(mesh):
    return jax.shard_map(
        local,
        mesh=mesh,
        in_specs=(
            P(("case", "blk", "split", "sub"), None, None),
            P(("case", "blk", "split", "sub")),
            P(("case", "blk", "split", "sub")),
            P(None, ("case", "blk", "split", "sub")),
            P(None, "case"),
        ),
        out_specs=P(("case", "blk"), None, None),
        check_vma=False,
    )
```

profile of v0, /device:TPU:0, one launch (start us, length us, event | category | flops | bytes accessed | tf_op | source)
XLA Modules:
  0.0 115.6 jit_solution(8116364706808095267)
XLA Ops:
  6.5 0.7 add_select_fusion.1
  7.9 2.3 %reduce-window.6 = s32[8,8,128]{2,1,0:T(8,128)S(1)} reduce-window(s32[8,8,128]{2,1,0:T(8,128)S(1)} %fusion.62, s32[]{:T(128)} %constant.50.clone.1), window={size=1x1x128 pad=0_0x0_0x127_0}, to_apply=%region_0.1 | reduce-window | flops 1040384 | bytes 65540 | tf_op jit(solution)/shard_map/reduce-window
  10.8 4.3 %scatter_custom_fusion = s32[1537]{0:T(1024)S(1)} fusion(s32[1024]{0:T(1024)S(1)} %compare_select_fusion.3, s32[1024]{0:T(1024)S(1)} %iota.57, s32[]{:T(128)} %constant.46.clone.1), kind=kCustom, calls=%fused_computation.159 | custom fusion | bytes 6152 | tf_op jit(solution)/shard_map/scatter | solution.py:93
  15.1 5.9 %gather_fusion.1 = s32[1536]{0:T(1024)S(1)} fusion(s32[1024]{0:T(1024)S(1)} %get-tuple-element.94, s32[2048]{0:T(1024)S(1)} %pad_clamp_fusion), kind=kCustom, calls=%fused_computation.1 | custom fusion | bytes 18432 | tf_op jit(solution)/shard_map/jit(_take)/gather | solution.py:95
  21.1 0.6 and_select_fusion
  21.8 7.3 %all-to-all-start.1 = ((s32[8,1,192]{2,1,0:T(1,128)}), s32[8,1,192]{2,1,0:T(1,128)S(1)}, u32[]{:S(2)}, u32[]{:S(2)}) async-start(s32[8,1,192]{2,1,0:T(1,128)} %and_select_fusion), calls=%async_computation.1 | async-start | bytes 16384 | tf_op jit(solution)/shard_map/all_to_all | solution.py:101
  29.3 3.4 %fusion.5 = f32[1024,16,4]{0,1,2:T(8,128)S(1)} fusion(bf16[1024,4,512]{2,1,0:T(4,128)(2,1)} %param.5, bf16[8,512]{1,0:T(8,128)(2,1)S(1)} %get-tuple-element.97, bf16[8,512]{1,0:T(8,128)(2,1)S(1)} %get-tuple-element.96), kind=kOutput, calls=%fused_computation.8 | convolution fusion | flops 67141632 | bytes 4472832 | tf_op jit(solution)/shard_map/jt,rt->jr/dot_general | solution.py:97
  33.2 2.6 %gather_fusion = f32[1536,64]{1,0:T(8,128)S(1)} fusion(f32[1024,64]{1,0:T(8,128)S(1)} %copy.23, s32[2048]{0:T(1024)S(1)} %pad_clamp_fusion), kind=kCustom, calls=%fused_computation | custom fusion | bytes 792576 | tf_op jit(solution)/shard_map/jit(_take)/gather | solution.py:99
  35.8 0.3 copy.24
  36.2 0.8 broadcast_select_fusion
  37.0 6.0 %all-to-all-start = ((f32[8,192,64]{1,2,0:T(8,128)}), f32[8,192,64]{1,2,0:T(8,128)S(1)}, u32[]{:S(2)}, u32[]{:S(2)}) async-start(f32[8,192,64]{1,2,0:T(8,128)} %broadcast_select_fusion), calls=%async_computation | async-start | bytes 1048576 | tf_op jit(solution)/shard_map/all_to_all | solution.py:108
  43.2 13.8 %all-to-all-done = f32[8,192,64]{1,2,0:T(8,128)S(1)} async-done(((f32[8,192,64]{1,2,0:T(8,128)}), f32[8,192,64]{1,2,0:T(8,128)S(1)}, u32[]{:S(2)}, u32[]{:S(2)}) %all-to-all-start) | async-done | bytes 393248 | tf_op jit(solution)/shard_map/all_to_all | solution.py:108
  57.6 0.8 fusion.3
  58.5 3.3 %multiply_reduce_fusion.8 = (f32[512]{0:T(512)S(1)}, f32[512]{0:T(512)S(1)}) fusion(f32[256]{0:T(256)S(1)} %bitcast.252, f32[512]{0:T(512)S(1)} %bitcast.156, f32[256]{0:T(256)S(1)} %bitcast.260, f32[512]{0:T(512)S(1)} %bitcast.164, f32[256]{0:T(256)S(1)} %bitcast.244, f32[512]{0:T(512)S(1)} %bitcast.148, f32[256]{0:T(256)S(1)} %bitcast.229, ...), kind=kLoop, calls=%fused_computation.27 | loop fusion | flops 5635072 | bytes 22528 | tf_op jit(solution)/shard_map/reduce_sum | solution.py:60
  61.8 3.1 %multiply_reduce_fusion.9 = (f32[512]{0:T(512)S(1)}, f32[512]{0:T(512)S(1)}) fusion(f32[256]{0:T(256)S(1)} %bitcast.253, f32[512]{0:T(512)S(1)} %bitcast.157, f32[256]{0:T(256)S(1)} %bitcast.261, f32[512]{0:T(512)S(1)} %bitcast.165, f32[256]{0:T(256)S(1)} %bitcast.245, f32[512]{0:T(512)S(1)} %bitcast.149, f32[256]{0:T(256)S(1)} %bitcast.221, ...), kind=kLoop, calls=%fused_computation.32 | loop fusion | flops 5635072 | bytes 22528 | tf_op jit(solution)/shard_map/reduce_sum | solution.py:60
  64.9 3.1 %multiply_reduce_fusion.10 = (f32[512]{0:T(512)S(1)}, f32[512]{0:T(512)S(1)}) fusion(f32[256]{0:T(256)S(1)} %bitcast.254, f32[512]{0:T(512)S(1)} %bitcast.158, f32[256]{0:T(256)S(1)} %bitcast.262, f32[512]{0:T(512)S(1)} %bitcast.166, f32[256]{0:T(256)S(1)} %bitcast.246, f32[512]{0:T(512)S(1)} %bitcast.150, f32[256]{0:T(256)S(1)} %bitcast.213, ...), kind=kLoop, calls=%fused_computation.37 | loop fusion | flops 5635072 | bytes 22528 | tf_op jit(solution)/shard_map/reduce_sum | solution.py:60
  68.0 3.1 %multiply_reduce_fusion.11 = (f32[512]{0:T(512)S(1)}, f32[512]{0:T(512)S(1)}) fusion(f32[256]{0:T(256)S(1)} %bitcast.255, f32[512]{0:T(512)S(1)} %bitcast.159, f32[256]{0:T(256)S(1)} %bitcast.263, f32[512]{0:T(512)S(1)} %bitcast.167, f32[256]{0:T(256)S(1)} %bitcast.247, f32[512]{0:T(512)S(1)} %bitcast.151, f32[256]{0:T(256)S(1)} %bitcast.205, ...), kind=kLoop, calls=%fused_computation.82 | loop fusion | flops 5635072 | bytes 22528 | tf_op jit(solution)/shard_map/reduce_sum | solution.py:60
  71.1 3.1 %multiply_reduce_fusion.12 = (f32[512]{0:T(512)S(1)}, f32[512]{0:T(512)S(1)}) fusion(f32[256]{0:T(256)S(1)} %bitcast.256, f32[512]{0:T(512)S(1)} %bitcast.160, f32[256]{0:T(256)S(1)} %bitcast.264, f32[512]{0:T(512)S(1)} %bitcast.168, f32[256]{0:T(256)S(1)} %bitcast.248, f32[512]{0:T(512)S(1)} %bitcast.152, f32[256]{0:T(256)S(1)} %bitcast.197, ...), kind=kLoop, calls=%fused_computation.85 | loop fusion | flops 5635072 | bytes 22528 | tf_op jit(solution)/shard_map/reduce_sum | solution.py:60
  74.2 3.0 %multiply_reduce_fusion.13 = (f32[512]{0:T(512)S(1)}, f32[512]{0:T(512)S(1)}) fusion(f32[256]{0:T(256)S(1)} %bitcast.257, f32[512]{0:T(512)S(1)} %bitcast.161, f32[256]{0:T(256)S(1)} %bitcast.265, f32[512]{0:T(512)S(1)} %bitcast.169, f32[256]{0:T(256)S(1)} %bitcast.249, f32[512]{0:T(512)S(1)} %bitcast.153, f32[256]{0:T(256)S(1)} %bitcast.189, ...), kind=kLoop, calls=%fused_computation.88 | loop fusion | flops 5241856 | bytes 22528 | tf_op jit(solution)/shard_map/reduce_sum | solution.py:60
  77.2 3.1 %multiply_reduce_fusion.14 = (f32[512]{0:T(512)S(1)}, f32[512]{0:T(512)S(1)}) fusion(f32[256]{0:T(256)S(1)} %bitcast.258, f32[512]{0:T(512)S(1)} %bitcast.162, f32[256]{0:T(256)S(1)} %bitcast.266, f32[512]{0:T(512)S(1)} %bitcast.170, f32[256]{0:T(256)S(1)} %bitcast.250, f32[512]{0:T(512)S(1)} %bitcast.154, f32[256]{0:T(256)S(1)} %bitcast.181, ...), kind=kLoop, calls=%fused_computation.91 | loop fusion | flops 5635072 | bytes 22528 | tf_op jit(solution)/shard_map/reduce_sum | solution.py:60
  80.3 3.1 %multiply_reduce_fusion.15 = (f32[512]{0:T(512)S(1)}, f32[512]{0:T(512)S(1)}) fusion(f32[256]{0:T(256)S(1)} %bitcast.259, f32[512]{0:T(512)S(1)} %bitcast.163, f32[256]{0:T(256)S(1)} %bitcast.267, f32[512]{0:T(512)S(1)} %bitcast.171, f32[256]{0:T(256)S(1)} %bitcast.251, f32[512]{0:T(512)S(1)} %bitcast.155, f32[256]{0:T(256)S(1)} %bitcast.173, ...), kind=kLoop, calls=%fused_computation.94 | loop fusion | flops 5635072 | bytes 22528 | tf_op jit(solution)/shard_map/reduce_sum | solution.py:60
  83.5 0.6 pad_maximum_fusion
  84.1 18.1 %reduce-scatter.2.cloned.1.call-done = f32[128,2,8]{0,2,1:T(8,128)} async-done(((f32[512,2,8]{0,2,1:T(8,128)}), f32[128,2,8]{0,2,1:T(8,128)}) %reduce-scatter.2.cloned.1.call-update) | async-done | bytes 8208 | tf_op jit(solution)/shard_map/reduce_scatter | solution.py:126
  102.3 6.4 %psum.7 = f32[128,2,8]{0,2,1:T(8,128)} all-reduce(f32[128,2,8]{0,2,1:T(8,128)} %reduce-scatter.2.cloned.1.call-done), channel_id=1, replica_groups=mesh['case'=2,'blk'=4,'split'=2,'sub'=2] {'split','sub'}, use_global_device_ids=true, to_apply=%region_21.22 | all-reduce | flops 2048 | bytes 16384 | tf_op jit(solution)/shard_map/psum | solution.py:129
  (41 shorter events, 2.4 us)
Async XLA Ops:
  21.8 15.2 %all-to-all-start.1 = ((s32[8,1,192]{2,1,0:T(1,128)}), s32[8,1,192]{2,1,0:T(1,128)S(1)}, u32[]{:S(2)}, u32[]{:S(2)}) async-start(s32[8,1,192]{2,1,0:T(1,128)} %and_select_fusion), calls=%async_computation.1 | async-start | bytes 16384 | tf_op jit(solution)/shard_map/all_to_all | solution.py:101
  33.2 9.9 %copy-start.1 = (f32[4,256]{1,0:T(4,128)S(1)}, f32[4,256]{1,0:T(4,128)}, u32[]{:S(2)}) copy-start(f32[4,256]{1,0:T(4,128)} %param.8) | copy-start | bytes 12292
  33.2 9.9 %copy-start = (f32[3,512]{1,0:T(4,128)S(1)}, f32[3,512]{1,0:T(4,128)}, u32[]{:S(2)}) copy-start(f32[3,512]{1,0:T(4,128)} %param.9) | copy-start | bytes 18436
  37.0 20.0 %all-to-all-start = ((f32[8,192,64]{1,2,0:T(8,128)}), f32[8,192,64]{1,2,0:T(8,128)S(1)}, u32[]{:S(2)}, u32[]{:S(2)}) async-start(f32[8,192,64]{1,2,0:T(8,128)} %broadcast_select_fusion), calls=%async_computation | async-start | bytes 1048576 | tf_op jit(solution)/shard_map/all_to_all | solution.py:108
  43.0 59.3 %reduce-scatter.2.cloned.1.call-start = ((), (), s32[]{:S(2)}) async-start(), calls=%async_computation.3 | async-start | bytes 40960 | tf_op jit(solution)/shard_map/reduce_scatter | solution.py:126
Sparse Core Ops, SparseCore 0:
  84.3 17.9 reduce-scatter.1
where the time goes:
time: 116 us
  waiting for transfers between devices  31.9 us (28%)
  other arithmetic  30.6 us (26%)
  local copies, waits for them, and re-layouts  14.8 us (13%)
  between operations  14.3 us (12%)
  starting transfers between devices  13.3 us (11%)
  blocking collectives  6.44 us (6%)
  matrix products  4.22 us (4%)
    reduce_sum x8, other arithmetic, radiate(): jnp.sum(quadrature_factor * (source_real * cosine + source_imag * sinusoi...  24.9 us
    reduce_scatter x1, waiting for transfers between devices, local(): lax.psum_scatter(radiate(spectra, surface, observers, amplitude), 'blk',...  18.1 us
    all_to_all x1, waiting for transfers between devices, local(): lax.all_to_all(outgoing.reshape(source_groups, capacity, 8 * NF), ('blk',...  13.8 us
    all_to_all x1, starting transfers between devices, local(): lax.all_to_all(slot_point.reshape(source_groups, capacity), ('blk', 'spli...  7.25 us
    psum x1, blocking collectives, local(): return lax.psum(summed, ('split', 'sub'))  6.44 us
    all_to_all x1, starting transfers between devices, local(): lax.all_to_all(outgoing.reshape(source_groups, capacity, 8 * NF), ('blk',...  6 us
    gather x2, local copies, waits for them, and re-layouts, local(): slot_point = jnp.take(point_index, slot_source, mode='fill', fill_value=-1)  5.93 us
    scatter x1, local copies, waits for them, and re-layouts, local(): jnp.full((slot_total + 1,), rows_dev, jnp.int32).at[destination]  4.32 us
  transfers between devices with their start and end apart: 3, of which 2 were waited for; matrix products, arithmetic and copies ran while one was open for 7% of the time, Pallas kernels for 0%

commit v1 on v0

--- a/solution.py
+++ b/solution.py
@@ -5,6 +5,10 @@
 from jax.sharding import PartitionSpec as P
 
 NF = 8
+
+
+def state_the_skins(local_x, mesh_dim, row_axis):
+    return lax.psum(lax.psum(local_x, mesh_dim), row_axis)
 
 
 def spectral_lookup_matrix(signal_readings):
@@ -126,7 +130,7 @@
     summed = lax.psum_scatter(
         radiate(spectra, surface, observers, amplitude), "blk", scatter_dimension=0, tiled=True
     )
-    return lax.psum(summed, ("split", "sub"))
+    return state_the_skins(summed, "sub", "split")
 
 
 def solution(mesh):

time: 116 us -> 118 us (1.017)
  blocking collectives: 6.44 us -> 8.16 us
    psum x1 -> x2, blocking collectives: 6.44 us -> 8.16 us  [state_the_skins(): return lax.psum(lax.psum(local_x, mesh_dim), row_axis)]
where the time goes in v1:
time: 118 us; the launch traced here: 117 us
  waiting for transfers between devices  31.9 us (27%)
  other arithmetic  30.6 us (26%)
  local copies, waits for them, and re-layouts  14.8 us (13%)
  between operations  14.3 us (12%)
  starting transfers between devices  13.3 us (11%)
  blocking collectives  8.16 us (7%)
  matrix products  4.22 us (4%)
    reduce_sum x8, other arithmetic, radiate(): jnp.sum(quadrature_factor * (source_real * cosine + source_imag * sinusoi...  24.9 us
    reduce_scatter x1, waiting for transfers between devices, local(): lax.psum_scatter(radiate(spectra, surface, observers, amplitude), 'blk',...  18.1 us
    all_to_all x1, waiting for transfers between devices, local(): lax.all_to_all(outgoing.reshape(source_groups, capacity, 8 * NF), ('blk',...  13.8 us
    psum x2, blocking collectives, state_the_skins(): return lax.psum(lax.psum(local_x, mesh_dim), row_axis)  8.16 us
    all_to_all x1, starting transfers between devices, local(): lax.all_to_all(slot_point.reshape(source_groups, capacity), ('blk', 'spli...  7.25 us
    all_to_all x1, starting transfers between devices, local(): lax.all_to_all(outgoing.reshape(source_groups, capacity, 8 * NF), ('blk',...  6 us
    gather x2, local copies, waits for them, and re-layouts, local(): slot_point = jnp.take(point_index, slot_source, mode='fill', fill_value=-1)  5.93 us
    scatter x1, local copies, waits for them, and re-layouts, local(): jnp.full((slot_total + 1,), rows_dev, jnp.int32).at[destination]  4.32 us
  transfers between devices with their start and end apart: 3, of which 2 were waited for; matrix products, arithmetic and copies ran while one was open for 7% of the time, Pallas kernels for 0%

profile of v1, /device:TPU:0, one launch (start us, length us, event | category | flops | bytes accessed | tf_op | source)
XLA Modules:
  0.0 117.3 jit_solution(10347456890335686757)
XLA Ops:
  6.5 0.7 add_select_fusion.1
  7.9 2.3 %reduce-window.6 = s32[8,8,128]{2,1,0:T(8,128)S(1)} reduce-window(s32[8,8,128]{2,1,0:T(8,128)S(1)} %fusion.62, s32[]{:T(128)} %constant.50.clone.1), window={size=1x1x128 pad=0_0x0_0x127_0}, to_apply=%region_0.1 | reduce-window | flops 1040384 | bytes 65540 | tf_op jit(solution)/shard_map/reduce-window
  10.8 4.3 %scatter_custom_fusion = s32[1537]{0:T(1024)S(1)} fusion(s32[1024]{0:T(1024)S(1)} %compare_select_fusion.3, s32[1024]{0:T(1024)S(1)} %iota.57, s32[]{:T(128)} %constant.46.clone.1), kind=kCustom, calls=%fused_computation.159 | custom fusion | bytes 6152 | tf_op jit(solution)/shard_map/scatter | solution.py:97
  15.1 5.9 %gather_fusion.1 = s32[1536]{0:T(1024)S(1)} fusion(s32[1024]{0:T(1024)S(1)} %get-tuple-element.94, s32[2048]{0:T(1024)S(1)} %pad_clamp_fusion), kind=kCustom, calls=%fused_computation.1 | custom fusion | bytes 18432 | tf_op jit(solution)/shard_map/jit(_take)/gather | solution.py:99
  21.1 0.6 and_select_fusion
  21.8 7.3 %all-to-all-start.1 = ((s32[8,1,192]{2,1,0:T(1,128)}), s32[8,1,192]{2,1,0:T(1,128)S(1)}, u32[]{:S(2)}, u32[]{:S(2)}) async-start(s32[8,1,192]{2,1,0:T(1,128)} %and_select_fusion), calls=%async_computation.1 | async-start | bytes 16384 | tf_op jit(solution)/shard_map/all_to_all | solution.py:105
  29.3 3.4 %fusion.5 = f32[1024,16,4]{0,1,2:T(8,128)S(1)} fusion(bf16[1024,4,512]{2,1,0:T(4,128)(2,1)} %param.5, bf16[8,512]{1,0:T(8,128)(2,1)S(1)} %get-tuple-element.97, bf16[8,512]{1,0:T(8,128)(2,1)S(1)} %get-tuple-element.96), kind=kOutput, calls=%fused_computation.8 | convolution fusion | flops 67141632 | bytes 4472832 | tf_op jit(solution)/shard_map/jt,rt->jr/dot_general | solution.py:101
  33.2 2.6 %gather_fusion = f32[1536,64]{1,0:T(8,128)S(1)} fusion(f32[1024,64]{1,0:T(8,128)S(1)} %copy.23, s32[2048]{0:T(1024)S(1)} %pad_clamp_fusion), kind=kCustom, calls=%fused_computation | custom fusion | bytes 792576 | tf_op jit(solution)/shard_map/jit(_take)/gather | solution.py:103
  36.2 0.8 broadcast_select_fusion
  37.0 6.0 %all-to-all-start = ((f32[8,192,64]{1,2,0:T(8,128)}), f32[8,192,64]{1,2,0:T(8,128)S(1)}, u32[]{:S(2)}, u32[]{:S(2)}) async-start(f32[8,192,64]{1,2,0:T(8,128)} %broadcast_select_fusion), calls=%async_computation | async-start | bytes 1048576 | tf_op jit(solution)/shard_map/all_to_all | solution.py:112
  43.2 13.8 %all-to-all-done = f32[8,192,64]{1,2,0:T(8,128)S(1)} async-done(((f32[8,192,64]{1,2,0:T(8,128)}), f32[8,192,64]{1,2,0:T(8,128)S(1)}, u32[]{:S(2)}, u32[]{:S(2)}) %all-to-all-start) | async-done | bytes 393248 | tf_op jit(solution)/shard_map/all_to_all | solution.py:112
  57.6 0.8 fusion.3
  58.5 3.3 %multiply_reduce_fusion.8 = (f32[512]{0:T(512)S(1)}, f32[512]{0:T(512)S(1)}) fusion(f32[256]{0:T(256)S(1)} %bitcast.252, f32[512]{0:T(512)S(1)} %bitcast.156, f32[256]{0:T(256)S(1)} %bitcast.260, f32[512]{0:T(512)S(1)} %bitcast.164, f32[256]{0:T(256)S(1)} %bitcast.244, f32[512]{0:T(512)S(1)} %bitcast.148, f32[256]{0:T(256)S(1)} %bitcast.229, ...), kind=kLoop, calls=%fused_computation.27 | loop fusion | flops 5635072 | bytes 22528 | tf_op jit(solution)/shard_map/reduce_sum | solution.py:64
  61.8 3.1 %multiply_reduce_fusion.9 = (f32[512]{0:T(512)S(1)}, f32[512]{0:T(512)S(1)}) fusion(f32[256]{0:T(256)S(1)} %bitcast.253, f32[512]{0:T(512)S(1)} %bitcast.157, f32[256]{0:T(256)S(1)} %bitcast.261, f32[512]{0:T(512)S(1)} %bitcast.165, f32[256]{0:T(256)S(1)} %bitcast.245, f32[512]{0:T(512)S(1)} %bitcast.149, f32[256]{0:T(256)S(1)} %bitcast.221, ...), kind=kLoop, calls=%fused_computation.32 | loop fusion | flops 5635072 | bytes 22528 | tf_op jit(solution)/shard_map/reduce_sum | solution.py:64
  64.9 3.1 %multiply_reduce_fusion.10 = (f32[512]{0:T(512)S(1)}, f32[512]{0:T(512)S(1)}) fusion(f32[256]{0:T(256)S(1)} %bitcast.254, f32[512]{0:T(512)S(1)} %bitcast.158, f32[256]{0:T(256)S(1)} %bitcast.262, f32[512]{0:T(512)S(1)} %bitcast.166, f32[256]{0:T(256)S(1)} %bitcast.246, f32[512]{0:T(512)S(1)} %bitcast.150, f32[256]{0:T(256)S(1)} %bitcast.213, ...), kind=kLoop, calls=%fused_computation.37 | loop fusion | flops 5635072 | bytes 22528 | tf_op jit(solution)/shard_map/reduce_sum | solution.py:64
  68.0 3.1 %multiply_reduce_fusion.11 = (f32[512]{0:T(512)S(1)}, f32[512]{0:T(512)S(1)}) fusion(f32[256]{0:T(256)S(1)} %bitcast.255, f32[512]{0:T(512)S(1)} %bitcast.159, f32[256]{0:T(256)S(1)} %bitcast.263, f32[512]{0:T(512)S(1)} %bitcast.167, f32[256]{0:T(256)S(1)} %bitcast.247, f32[512]{0:T(512)S(1)} %bitcast.151, f32[256]{0:T(256)S(1)} %bitcast.205, ...), kind=kLoop, calls=%fused_computation.82 | loop fusion | flops 5635072 | bytes 22528 | tf_op jit(solution)/shard_map/reduce_sum | solution.py:64
  71.1 3.1 %multiply_reduce_fusion.12 = (f32[512]{0:T(512)S(1)}, f32[512]{0:T(512)S(1)}) fusion(f32[256]{0:T(256)S(1)} %bitcast.256, f32[512]{0:T(512)S(1)} %bitcast.160, f32[256]{0:T(256)S(1)} %bitcast.264, f32[512]{0:T(512)S(1)} %bitcast.168, f32[256]{0:T(256)S(1)} %bitcast.248, f32[512]{0:T(512)S(1)} %bitcast.152, f32[256]{0:T(256)S(1)} %bitcast.197, ...), kind=kLoop, calls=%fused_computation.85 | loop fusion | flops 5635072 | bytes 22528 | tf_op jit(solution)/shard_map/reduce_sum | solution.py:64
  74.2 3.0 %multiply_reduce_fusion.13 = (f32[512]{0:T(512)S(1)}, f32[512]{0:T(512)S(1)}) fusion(f32[256]{0:T(256)S(1)} %bitcast.257, f32[512]{0:T(512)S(1)} %bitcast.161, f32[256]{0:T(256)S(1)} %bitcast.265, f32[512]{0:T(512)S(1)} %bitcast.169, f32[256]{0:T(256)S(1)} %bitcast.249, f32[512]{0:T(512)S(1)} %bitcast.153, f32[256]{0:T(256)S(1)} %bitcast.189, ...), kind=kLoop, calls=%fused_computation.88 | loop fusion | flops 5241856 | bytes 22528 | tf_op jit(solution)/shard_map/reduce_sum | solution.py:64
  77.2 3.1 %multiply_reduce_fusion.14 = (f32[512]{0:T(512)S(1)}, f32[512]{0:T(512)S(1)}) fusion(f32[256]{0:T(256)S(1)} %bitcast.258, f32[512]{0:T(512)S(1)} %bitcast.162, f32[256]{0:T(256)S(1)} %bitcast.266, f32[512]{0:T(512)S(1)} %bitcast.170, f32[256]{0:T(256)S(1)} %bitcast.250, f32[512]{0:T(512)S(1)} %bitcast.154, f32[256]{0:T(256)S(1)} %bitcast.181, ...), kind=kLoop, calls=%fused_computation.91 | loop fusion | flops 5635072 | bytes 22528 | tf_op jit(solution)/shard_map/reduce_sum | solution.py:64
  80.3 3.1 %multiply_reduce_fusion.15 = (f32[512]{0:T(512)S(1)}, f32[512]{0:T(512)S(1)}) fusion(f32[256]{0:T(256)S(1)} %bitcast.259, f32[512]{0:T(512)S(1)} %bitcast.163, f32[256]{0:T(256)S(1)} %bitcast.267, f32[512]{0:T(512)S(1)} %bitcast.171, f32[256]{0:T(256)S(1)} %bitcast.251, f32[512]{0:T(512)S(1)} %bitcast.155, f32[256]{0:T(256)S(1)} %bitcast.173, ...), kind=kLoop, calls=%fused_computation.94 | loop fusion | flops 5635072 | bytes 22528 | tf_op jit(solution)/shard_map/reduce_sum | solution.py:64
  83.5 0.6 pad_maximum_fusion
  84.1 18.1 %reduce-scatter.2.cloned.1.call-done = f32[128,2,8]{0,2,1:T(8,128)} async-done(((f32[512,2,8]{0,2,1:T(8,128)}), f32[128,2,8]{0,2,1:T(8,128)}) %reduce-scatter.2.cloned.1.call-update) | async-done | bytes 8208 | tf_op jit(solution)/shard_map/reduce_scatter | solution.py:130
  102.3 2.6 %psum.14 = f32[128,2,8]{0,2,1:T(8,128)S(1)} all-reduce(f32[128,2,8]{0,2,1:T(8,128)} %reduce-scatter.2.cloned.1.call-done), channel_id=1, replica_groups=mesh['case'=2,'blk'=4,'split'=2,'sub'=2] {'sub'}, use_global_device_ids=true, to_apply=%region_21.22 | all-reduce | flops 2048 | bytes 16384 | tf_op jit(solution)/shard_map/psum | solution.py:11
  104.9 5.6 %psum.15 = f32[128,2,8]{0,2,1:T(8,128)} all-reduce(f32[128,2,8]{0,2,1:T(8,128)S(1)} %psum.14), channel_id=1, replica_groups=mesh['case'=2,'blk'=4,'split'=2,'sub'=2] {'split'}, use_global_device_ids=true, to_apply=%region_22.23 | all-reduce | flops 2048 | bytes 16384 | tf_op jit(solution)/shard_map/psum | solution.py:11
  (42 shorter events, 2.7 us)
Async XLA Ops:
  21.8 15.2 %all-to-all-start.1 = ((s32[8,1,192]{2,1,0:T(1,128)}), s32[8,1,192]{2,1,0:T(1,128)S(1)}, u32[]{:S(2)}, u32[]{:S(2)}) async-start(s32[8,1,192]{2,1,0:T(1,128)} %and_select_fusion), calls=%async_computation.1 | async-start | bytes 16384 | tf_op jit(solution)/shard_map/all_to_all | solution.py:105
  33.2 9.9 %copy-start.1 = (f32[4,256]{1,0:T(4,128)S(1)}, f32[4,256]{1,0:T(4,128)}, u32[]{:S(2)}) copy-start(f32[4,256]{1,0:T(4,128)} %param.8) | copy-start | bytes 12292
  33.2 9.9 %copy-start = (f32[3,512]{1,0:T(4,128)S(1)}, f32[3,512]{1,0:T(4,128)}, u32[]{:S(2)}) copy-start(f32[3,512]{1,0:T(4,128)} %param.9) | copy-start | bytes 18436
  37.0 20.0 %all-to-all-start = ((f32[8,192,64]{1,2,0:T(8,128)}), f32[8,192,64]{1,2,0:T(8,128)S(1)}, u32[]{:S(2)}, u32[]{:S(2)}) async-start(f32[8,192,64]{1,2,0:T(8,128)} %broadcast_select_fusion), calls=%async_computation | async-start | bytes 1048576 | tf_op jit(solution)/shard_map/all_to_all | solution.py:112
  43.0 59.3 %reduce-scatter.2.cloned.1.call-start = ((), (), s32[]{:S(2)}) async-start(), calls=%async_computation.3 | async-start | bytes 40960 | tf_op jit(solution)/shard_map/reduce_scatter | solution.py:130
Sparse Core Ops, SparseCore 0:
  84.3 17.9 reduce-scatter.1
